TPU v7x, 32 devices: a whole 2x2x4 slice. The times are simulated.
32 devices in a mesh: cols: 8 (over y, x, core), rows: 4 (over z).
Axes of the slice: x: 2, y: 2, z: 4, core: 2. Of those that a mesh axis runs over, the one named last changes fastest.
Arguments:
- weight: float32 [8192, 26, 1024], P('rows', None, 'cols'), may hold values from -6 to 6
- factor_rows: bfloat16 [1024, 26, 1024], P('rows', None, 'cols'), may hold values from -0.1875 to 0.1875
- diag_inverse: float32 [8, 128, 128], replicated, may hold values from -1 to 2, as said below
- keep_codes: int32 [8192, 256], P('rows'), may hold values from 0 to 5
- block_order: int32 [8], replicated, may hold values from 0 to 7, each once
Outputs:
- pruned: float32 [8192, 26, 1024], P('rows', None, 'cols')
Inputs may be any that keep to these rules, and one draw needn't show every extreme that they name: `block_order`: each entry of 0 to 7 appears once. `diag_inverse`: upper triangular with diagonal entries of 1 to 2.
All inputs are finite; a program needn't handle non-finite values.
Results may differ from a plain program's by a relative error of at most 0.0028.
Values may be sent and summed in bfloat16 or wider, within the bound.
A program may use at most 128 MiB of HBM per device.

v0:
```python
import jax
import jax.numpy as jnp
import numpy as np
from jax import lax
from jax.sharding import PartitionSpec as P

BLOCKS = 8


pair_table = np.array(
    [[1, 1, 0, 0], [1, 0, 1, 0], [1, 0, 0, 1], [0, 1, 1, 0], [0, 1, 0, 1], [0, 0, 1, 1]],
    dtype=np.float32,
)


def spread(shard, axis, root):
    mine = lax.axis_index(axis) == root
    return lax.psum(jnp.where(mine, shard, jnp.zeros_like(shard)), axis)


def decode(codes):
    onehot = (codes[:, :, None] == jnp.arange(6, dtype=jnp.int32)).astype(jnp.float32)
    kept_mask = jnp.einsum("rgo,ok->rgk", onehot, jnp.asarray(pair_table, dtype=jnp.float32))
    return kept_mask.reshape(codes.shape[0], -1)


def body(weight, factor_rows, diag_inverse, keep_codes, block_order):
    column_count = lax.axis_size("cols")
    my_column = lax.axis_index("cols")
    lap_count = weight.shape[1]
    tile_width = weight.shape[2]
    lap_ids = jnp.arange(lap_count, dtype=jnp.int32)
    block_ids = lap_ids * column_count + my_column
    all_factor = lax.all_gather(factor_rows, "rows", axis=0, tiled=True)

    def errors(matrix, block_now):
        lap_index = block_now // column_count
        block_vals = lax.dynamic_index_in_dim(matrix, lap_index, 1, False)
        kept_mask = decode(lax.dynamic_slice_in_dim(keep_codes, block_now * 32, 32, 1))
        errors_bf = jnp.dot(
            block_vals * (1.0 - kept_mask),
            diag_inverse[block_now],
            precision=lax.Precision.HIGHEST,
            preferred_element_type=jnp.float32,
        ).astype(jnp.bfloat16)
        errors_bf = spread(errors_bf, "cols", block_now - lap_index * column_count)
        return (errors_bf, block_vals * kept_mask)

    matrix = weight
    finished = jnp.zeros((lap_count,), dtype=bool)
    errors_bf, kept_block = errors(matrix, block_order[0])
    for step_index in range(BLOCKS):
        block_now = block_order[step_index]
        lap_index = block_now // column_count
        factor_tile = lax.dynamic_slice_in_dim(all_factor, block_now * tile_width, tile_width, 0)
        finished = jnp.logical_or(finished, block_ids == block_now)
        holder_here = my_column == block_now - lap_index * column_count
        previous = lax.dynamic_index_in_dim(matrix, lap_index, 1, False)
        matrix = lax.dynamic_update_index_in_dim(
            matrix, jnp.where(holder_here, kept_block, previous), lap_index, 1
        )
        pending = jnp.logical_not(finished)
        product = jnp.dot(
            errors_bf, factor_tile.reshape(tile_width, -1), preferred_element_type=jnp.float32
        )
        matrix = jnp.where(
            pending[None, :, None],
            matrix - product.reshape(errors_bf.shape[0], lap_count, tile_width),
            matrix,
        )
        if step_index + 1 < BLOCKS:
            errors_bf, kept_block = errors(matrix, block_order[step_index + 1])
    return matrix


def solution(mesh):
    in_specs = (P("rows", None, "cols"), P("rows", None, "cols"), P(), P("rows", None), P())
    out_specs = P("rows", None, "cols")
    return jax.shard_map(body, mesh=mesh, in_specs=in_specs, out_specs=out_specs, check_vma=False)
```

profile of v0, /device:TPU:0, one launch (start us, length us, event | category | flops | bytes accessed | tf_op | source)
XLA Modules:
  0.0 742.2 jit_solution(5922567340163280190)
XLA Ops:
  7.4 20.7 %copy.73 = f32[2048,26,128]{2,0,1:T(8,128)} copy(f32[2048,26,128]{2,0,1:T(8,128)} %param.13) | data formatting | bytes 54525952
  37.1 5.5 constant_dynamic-slice_fusion.3
  49.1 3.0 fusion
  52.2 3.8 copy.34
  88.2 2.6 copy.54
  105.7 2.6 reshape.218
  113.8 2.6 reshape.216
  130.1 2.6 reshape.212
  147.8 5.5 or_not_fusion
  157.2 24.9 %all-gather.2.cloned.1.call-done = bf16[1024,26,128]{0,2,1:T(8,128)(2,1)} async-done(((bf16[256,26,128]{0,2,1:T(8,128)(2,1)}), bf16[1024,26,128]{0,2,1:T(8,128)(2,1)}) %all-gather.2.cloned.1.call-update) | async-done | bytes 6815760 | tf_op jit(solution)/shard_map/all_gather | solution.py:34
  182.1 19.3 %subtract_select_fusion.7 = f32[2048,26,128]{2,0,1:T(8,128)} fusion(f32[2048,26,128]{2,0,1:T(8,128)} %fusion.16, pred[26]{0:T(512)(128)(4,1)S(1)} %compare_not_fusion, bf16[1024,26,128]{0,2,1:T(8,128)(2,1)} %all-gather.2.cloned.1.call-done, s32[]{:T(128)S(6)} %select_n.289, bf16[2048,128]{1,0:T(8,128)(2,1)} %all-reduce.9.cloned.1.call-done), kind=kOutput, calls=%fused_computation.7 | convolution fusion | flops 1758461952 | bytes 55902240 | tf_op jit(solution)/shard_map/dot_general | solution.py:63
  201.4 3.0 fusion.1
  206.8 50.5 %all-reduce.11.cloned.1.call-done = bf16[2048,128]{1,0:T(8,128)(2,1)} async-done(((bf16[2048,128]{1,0:T(8,128)(2,1)}), bf16[2048,128]{1,0:T(8,128)(2,1)}) %all-reduce.11.cloned.1.call-update) | async-done | bytes 524304 | tf_op jit(solution)/shard_map/psum | solution.py:18
  257.4 19.2 %subtract_select_fusion.6 = f32[2048,26,128]{2,0,1:T(8,128)} fusion(f32[2048,26,128]{2,0,1:T(8,128)} %fusion.17, pred[26]{0:T(512)(128)(4,1)S(1)} %fusion.139, bf16[1024,26,128]{0,2,1:T(8,128)(2,1)} %all-gather.2.cloned.1.call-done, s32[]{:T(128)S(6)} %select_n.299, bf16[2048,128]{1,0:T(8,128)(2,1)} %all-reduce.11.cloned.1.call-done), kind=kOutput, calls=%fused_computation.6 | convolution fusion | flops 1758461952 | bytes 55902240 | tf_op jit(solution)/shard_map/dot_general | solution.py:63
  276.6 3.0 fusion.2
  282.0 51.6 %all-reduce.13.cloned.1.call-done = bf16[2048,128]{1,0:T(8,128)(2,1)} async-done(((bf16[2048,128]{1,0:T(8,128)(2,1)}), bf16[2048,128]{1,0:T(8,128)(2,1)}) %all-reduce.13.cloned.1.call-update) | async-done | bytes 524304 | tf_op jit(solution)/shard_map/psum | solution.py:18
  333.6 19.1 %subtract_select_fusion.5 = f32[2048,26,128]{2,0,1:T(8,128)} fusion(f32[2048,26,128]{2,0,1:T(8,128)} %fusion.18, pred[26]{0:T(512)(128)(4,1)S(1)} %fusion.136, bf16[1024,26,128]{0,2,1:T(8,128)(2,1)} %all-gather.2.cloned.1.call-done, s32[]{:T(128)S(6)} %select_n.309, bf16[2048,128]{1,0:T(8,128)(2,1)} %all-reduce.13.cloned.1.call-done), kind=kOutput, calls=%fused_computation.5 | convolution fusion | flops 1758461952 | bytes 55902240 | tf_op jit(solution)/shard_map/dot_general | solution.py:63
  352.7 3.0 fusion.3
  358.1 51.7 %all-reduce.15.cloned.1.call-done = bf16[2048,128]{1,0:T(8,128)(2,1)} async-done(((bf16[2048,128]{1,0:T(8,128)(2,1)}), bf16[2048,128]{1,0:T(8,128)(2,1)}) %all-reduce.15.cloned.1.call-update) | async-done | bytes 524304 | tf_op jit(solution)/shard_map/psum | solution.py:18
  409.7 19.5 %subtract_select_fusion.4 = f32[2048,26,128]{2,0,1:T(8,128)} fusion(f32[2048,26,128]{2,0,1:T(8,128)} %fusion.19, pred[26]{0:T(512)(128)(4,1)S(1)} %get-tuple-element.19, bf16[1024,26,128]{0,2,1:T(8,128)(2,1)} %all-gather.2.cloned.1.call-done, s32[]{:T(128)S(6)} %select_n.319, bf16[2048,128]{1,0:T(8,128)(2,1)} %all-reduce.15.cloned.1.call-done), kind=kOutput, calls=%fused_computation.4 | convolution fusion | flops 1758461952 | bytes 55902240 | tf_op jit(solution)/shard_map/dot_general | solution.py:63
  429.2 3.0 fusion.4
  434.6 51.6 %all-reduce.17.cloned.1.call-done = bf16[2048,128]{1,0:T(8,128)(2,1)} async-done(((bf16[2048,128]{1,0:T(8,128)(2,1)}), bf16[2048,128]{1,0:T(8,128)(2,1)}) %all-reduce.17.cloned.1.call-update) | async-done | bytes 524304 | tf_op jit(solution)/shard_map/psum | solution.py:18
  486.2 19.2 %subtract_select_fusion.3 = f32[2048,26,128]{2,0,1:T(8,128)} fusion(f32[2048,26,128]{2,0,1:T(8,128)} %fusion.20, pred[26]{0:T(512)(128)(4,1)S(1)} %get-tuple-element.18, bf16[1024,26,128]{0,2,1:T(8,128)(2,1)} %all-gather.2.cloned.1.call-done, s32[]{:T(128)S(6)} %select_n.329, bf16[2048,128]{1,0:T(8,128)(2,1)} %all-reduce.17.cloned.1.call-done), kind=kOutput, calls=%fused_computation.3 | convolution fusion | flops 1758461952 | bytes 55902240 | tf_op jit(solution)/shard_map/dot_general | solution.py:63
  505.4 3.0 fusion.5
  510.8 51.7 %all-reduce.19.cloned.1.call-done = bf16[2048,128]{1,0:T(8,128)(2,1)} async-done(((bf16[2048,128]{1,0:T(8,128)(2,1)}), bf16[2048,128]{1,0:T(8,128)(2,1)}) %all-reduce.19.cloned.1.call-update) | async-done | bytes 524304 | tf_op jit(solution)/shard_map/psum | solution.py:18
  562.5 19.3 %subtract_select_fusion.2 = f32[2048,26,128]{2,0,1:T(8,128)} fusion(f32[2048,26,128]{2,0,1:T(8,128)} %fusion.21, pred[26]{0:T(512)(128)(4,1)S(1)} %get-tuple-element.17, bf16[1024,26,128]{0,2,1:T(8,128)(2,1)} %all-gather.2.cloned.1.call-done, s32[]{:T(128)S(6)} %select_n.339, bf16[2048,128]{1,0:T(8,128)(2,1)} %all-reduce.19.cloned.1.call-done), kind=kOutput, calls=%fused_computation.2 | convolution fusion | flops 1758461952 | bytes 55902240 | tf_op jit(solution)/shard_map/dot_general | solution.py:63
  581.7 3.0 fusion.6
  587.1 51.7 %all-reduce.21.cloned.1.call-done = bf16[2048,128]{1,0:T(8,128)(2,1)} async-done(((bf16[2048,128]{1,0:T(8,128)(2,1)}), bf16[2048,128]{1,0:T(8,128)(2,1)}) %all-reduce.21.cloned.1.call-update) | async-done | bytes 524304 | tf_op jit(solution)/shard_map/psum | solution.py:18
  638.8 19.5 %subtract_select_fusion.1 = f32[2048,26,128]{2,0,1:T(8,128)} fusion(f32[2048,26,128]{2,0,1:T(8,128)} %fusion.22, pred[26]{0:T(512)(128)(4,1)S(1)} %copy-done.12, bf16[1024,26,128]{0,2,1:T(8,128)(2,1)} %all-gather.2.cloned.1.call-done, s32[]{:T(128)S(6)} %select_n.349, bf16[2048,128]{1,0:T(8,128)(2,1)} %all-reduce.21.cloned.1.call-done), kind=kOutput, calls=%fused_computation.1 | convolution fusion | flops 1758461952 | bytes 55902240 | tf_op jit(solution)/shard_map/dot_general | solution.py:63
  658.3 3.0 fusion.7
  663.6 51.7 %all-reduce.23.cloned.1.call-done = bf16[2048,128]{1,0:T(8,128)(2,1)} async-done(((bf16[2048,128]{1,0:T(8,128)(2,1)}), bf16[2048,128]{1,0:T(8,128)(2,1)}) %all-reduce.23.cloned.1.call-update) | async-done | bytes 524304 | tf_op jit(solution)/shard_map/psum | solution.py:18
  715.3 19.2 %subtract_select_fusion = f32[2048,26,128]{2,0,1:T(8,128)} fusion(f32[2048,26,128]{2,0,1:T(8,128)} %fusion.23, pred[26]{0:T(512)(128)(4,1)S(1)} %copy-done.11, bf16[1024,26,128]{0,2,1:T(8,128)(2,1)} %all-gather.2.cloned.1.call-done, s32[]{:T(128)S(6)} %select_n.359, bf16[2048,128]{1,0:T(8,128)(2,1)} %all-reduce.23.cloned.1.call-done), kind=kOutput, calls=%fused_computation | convolution fusion | flops 1758461952 | bytes 55902240 | tf_op jit(solution)/shard_map/dot_general | solution.py:63
  (87 shorter events, 73.3 us)
Async XLA Ops:
  7.4 41.7 %copy-start = (f32[8,128,128]{2,1,0:T(8,128)S(1)}, f32[8,128,128]{2,1,0:T(8,128)}, u32[]{:S(2)}) copy-start(f32[8,128,128]{2,1,0:T(8,128)} %param.15) | copy-start | bytes 1572868
  7.4 36.9 %copy-start.9 = (bf16[6,4,1]{0,1,2:T(4,128)(2,1)S(1)}, bf16[6,4,1]{0,1,2:T(4,128)(2,1)}, u32[]{:S(2)}) copy-start(bf16[6,4,1]{0,1,2:T(4,128)(2,1)} %constant.280) | copy-start | bytes 148
  7.4 29.8 %copy-start.1 = (s32[2048,256]{1,0:T(8,128)S(1)}, s32[2048,256]{1,0:T(8,128)}, u32[]{:S(2)}) copy-start(s32[2048,256]{1,0:T(8,128)} %param.16) | copy-start | bytes 6291460
  7.4 20.7 %copy-start.10 = (s32[8]{0:T(128)S(1)}, s32[8]{0:T(128)}, u32[]{:S(2)}) copy-start(s32[8]{0:T(128)} %param.17) | copy-start | bytes 100
  7.4 149.8 %all-reduce.9.cloned.1.call-start = ((), (), s32[]{:S(2)}) async-start(), calls=%async_computation | async-start | bytes 1048576 | tf_op jit(solution)/shard_map/psum | solution.py:18
  42.6 56.3 %copy-start.8 = (s32[2048,32]{1,0:T(8,128)S(1)}, s32[2048,32]{1,0:T(8,128)}, u32[]{:S(2)}) copy-start(s32[2048,32]{1,0:T(8,128)} %get-tuple-element.9) | copy-start | bytes 786436
  52.1 130.0 %all-gather.2.cloned.1.call-start = ((), (), s32[]{:S(2)}) async-start(), calls=%async_computation.1 | async-start | bytes 8519680 | tf_op jit(solution)/shard_map/all_gather | solution.py:34
  56.0 201.3 %all-reduce.11.cloned.1.call-start = ((), (), s32[]{:S(2)}) async-start(), calls=%async_computation.2 | async-start | bytes 1048576 | tf_op jit(solution)/shard_map/psum | solution.py:18
  157.2 44.2 %copy-start.7 = (f32[2048,1,128]{2,0,1:T(8,128)S(1)}, f32[2048,1,128]{2,0,1:T(8,128)}, u32[]{:S(2)}) copy-start(f32[2048,1,128]{2,0,1:T(8,128)} %copy.36) | copy-start | bytes 3145732
  204.5 129.1 %all-reduce.13.cloned.1.call-start = ((), (), s32[]{:S(2)}) async-start(), calls=%async_computation.3 | async-start | bytes 1048576 | tf_op jit(solution)/shard_map/psum | solution.py:18
  206.8 69.7 %copy-start.6 = (f32[2048,1,128]{2,0,1:T(8,128)S(1)}, f32[2048,1,128]{2,0,1:T(8,128)}, u32[]{:S(2)}) copy-start(f32[2048,1,128]{2,0,1:T(8,128)} %copy.39) | copy-start | bytes 3145732
  279.6 130.1 %all-reduce.15.cloned.1.call-start = ((), (), s32[]{:S(2)}) async-start(), calls=%async_computation.4 | async-start | bytes 1048576 | tf_op jit(solution)/shard_map/psum | solution.py:18
  282.0 70.7 %copy-start.5 = (f32[2048,1,128]{2,0,1:T(8,128)S(1)}, f32[2048,1,128]{2,0,1:T(8,128)}, u32[]{:S(2)}) copy-start(f32[2048,1,128]{2,0,1:T(8,128)} %copy.42) | copy-start | bytes 3145732
  355.7 130.5 %all-reduce.17.cloned.1.call-start = ((), (), s32[]{:S(2)}) async-start(), calls=%async_computation.5 | async-start | bytes 1048576 | tf_op jit(solution)/shard_map/psum | solution.py:18
  409.7 19.5 %copy-start.4 = (f32[2048,1,128]{2,0,1:T(8,128)S(1)}, f32[2048,1,128]{2,0,1:T(8,128)}, u32[]{:S(2)}) copy-start(f32[2048,1,128]{2,0,1:T(8,128)} %copy.45) | copy-start | bytes 3145732
  432.2 130.2 %all-reduce.19.cloned.1.call-start = ((), (), s32[]{:S(2)}) async-start(), calls=%async_computation.6 | async-start | bytes 1048576 | tf_op jit(solution)/shard_map/psum | solution.py:18
  508.4 130.3 %all-reduce.21.cloned.1.call-start = ((), (), s32[]{:S(2)}) async-start(), calls=%async_computation.7 | async-start | bytes 1048576 | tf_op jit(solution)/shard_map/psum | solution.py:18
  562.5 19.3 %copy-start.3 = (f32[2048,1,128]{2,0,1:T(8,128)S(1)}, f32[2048,1,128]{2,0,1:T(8,128)}, u32[]{:S(2)}) copy-start(f32[2048,1,128]{2,0,1:T(8,128)} %copy.51) | copy-start | bytes 3145732
  562.5 76.3 %copy-start.12 = (pred[26]{0:T(512)(128)(4,1)S(1)}, pred[26]{0:T(512)(128)(4,1)}, u32[]{:S(2)}) copy-start(pred[26]{0:T(512)(128)(4,1)} %get-tuple-element.16) | copy-start | bytes 82
  584.7 130.6 %all-reduce.23.cloned.1.call-start = ((), (), s32[]{:S(2)}) async-start(), calls=%async_computation.8 | async-start | bytes 1048576 | tf_op jit(solution)/shard_map/psum | solution.py:18
  638.8 19.5 %copy-start.2 = (f32[2048,1,128]{2,0,1:T(8,128)S(1)}, f32[2048,1,128]{2,0,1:T(8,128)}, u32[]{:S(2)}) copy-start(f32[2048,1,128]{2,0,1:T(8,128)} %copy.54) | copy-start | bytes 3145732
  638.8 76.5 %copy-start.11 = (pred[26]{0:T(512)(128)(4,1)S(1)}, pred[26]{0:T(512)(128)(4,1)}, u32[]{:S(2)}) copy-start(pred[26]{0:T(512)(128)(4,1)} %get-tuple-element.5) | copy-start | bytes 82
Sparse Core Ops, SparseCore 0:
  52.2 57.2 all-reduce.8
  204.6 52.7 all-reduce.10
  279.7 53.8 all-reduce.12
  355.8 53.8 all-reduce.14
  432.3 53.8 all-reduce.16
  508.5 53.8 all-reduce.18
  584.9 53.8 all-reduce.20
  661.4 53.8 all-reduce.22
Sparse Core Ops, SparseCore 1:
  56.1 125.9 all-gather.1
where the time goes:
time: 749 us; the launch traced here: 742 us
  waiting for transfers between devices  386 us (52%)
  matrix products  188 us (25%)
  local copies, waits for them, and re-layouts  78.6 us (10%)
  between operations  59.5 us (8%)
  other arithmetic  29.6 us (4%)
    psum x8, waiting for transfers between devices, spread(): return lax.psum(jnp.where(mine, shard, jnp.zeros_like(shard)), axis)  360 us
    dot_general x8, matrix products, body(): jnp.dot(errors_bf, factor_tile.reshape(tile_width, -1), preferred_element...  154 us
    reshape x16, local copies, waits for them, and re-layouts, decode(): return kept_mask.reshape(codes.shape[0], -1)  36.7 us
    all_gather x1, waiting for transfers between devices, body(): all_factor = lax.all_gather(factor_rows, 'rows', axis=0, tiled=True)  24.9 us
    unnamed x28, local copies, waits for them, and re-layouts  24.6 us
    dot_general x8, matrix products, errors(): jnp.dot(block_vals * (1.0 - kept_mask), diag_inverse[block_now], precisio...  24.1 us
    dynamic_update_slice x8, other arithmetic, body(): lax.dynamic_update_index_in_dim(matrix, jnp.where(holder_here, kept_block...  18.5 us
    dynamic_slice x9, local copies, waits for them, and re-layouts, errors(): lax.dynamic_slice_in_dim(keep_codes, block_now * 32, 32, 1)  16.6 us
  transfers between devices with their start and end apart: 9, of which 8 were waited for; matrix products, arithmetic and copies ran while one was open for 12% of the time, Pallas kernels for 0%

commit v1 on v0

v1 whole, which is shorter than its diff:
```python
import functools

import jax
import jax.numpy as jnp
from jax import lax
from jax.experimental import pallas as pl
from jax.experimental.pallas import tpu as pltpu
from jax.sharding import PartitionSpec as P

BLOCKS = 8
GROUP = 4


def keep_mask(codes, first_group, width):
    groups = codes.shape[1]
    row = lax.broadcasted_iota(jnp.int32, (groups, width), 0)
    column = lax.broadcasted_iota(jnp.int32, (groups, width), 1)
    pick = (row == first_group + column // GROUP).astype(jnp.float32).astype(jnp.bfloat16)
    spread_codes = jnp.dot(
        codes.astype(jnp.float32).astype(jnp.bfloat16), pick, preferred_element_type=jnp.float32
    )
    place = lax.broadcasted_iota(jnp.int32, (1, width), 1) % GROUP
    first = jnp.where(place < 2, 0.0, jnp.where(place == 2, 1.0, 2.0))
    second = jnp.where(place == 0, 1.0, jnp.where(place == 3, 4.0, 3.0))
    third = jnp.where(place == 0, 2.0, jnp.where(place == 1, 4.0, 5.0))
    hit = (spread_codes == first) | (spread_codes == second) | (spread_codes == third)
    return jnp.where(hit, 1.0, 0.0)


def chain_kernel(order_ref, block_ref, factor_ref, diag_ref, code_ref, error_ref, now):
    width = block_ref.shape[2]
    groups = code_ref.shape[1] // BLOCKS
    now[...] = block_ref[...]

    def step(s, carry):
        b = order_ref[s]
        kept = keep_mask(code_ref[...], b * groups, width)
        errors = jnp.dot(
            now[b] * (1.0 - kept),
            diag_ref[b],
            precision=lax.Precision.HIGHEST,
            preferred_element_type=jnp.float32,
        ).astype(jnp.bfloat16)
        start = pl.multiple_of(b * width, width)
        error_ref[:, pl.ds(start, width)] = errors
        for t in range(BLOCKS):
            now[t] -= jnp.dot(
                errors, factor_ref[t, pl.ds(start, width), :], preferred_element_type=jnp.float32
            )
        return carry

    lax.fori_loop(0, BLOCKS, step, 0)


def chain(order, blocks, factor, diag, codes):
    rows, width = blocks.shape[1:]
    whole = pl.BlockSpec(memory_space=pltpu.VMEM)
    return pl.pallas_call(
        chain_kernel,
        out_shape=jax.ShapeDtypeStruct((rows, BLOCKS * width), jnp.bfloat16),
        in_specs=[pl.BlockSpec(memory_space=pltpu.SMEM), whole, whole, whole, whole],
        out_specs=whole,
        scratch_shapes=[pltpu.VMEM(blocks.shape, jnp.float32)],
        compiler_params=pltpu.CompilerParams(vmem_limit_bytes=24 << 20),
        name="chain",
    )(order, blocks, factor, diag, codes)


def update_kernel(first, pair, rank_ref, error_ref, weight_ref, factor_ref, code_ref, *rest):
    out_ref = rest[-1]
    width = weight_ref.shape[2]

    def run(own):
        tiles = [factor_ref[i] for i in range(pair)]
        if own:
            depth = tiles[0].shape[0]
            column = rank_ref[BLOCKS]
            pruned = column < BLOCKS
            mine = jnp.where(pruned, rank_ref[jnp.minimum(column, BLOCKS - 1)], BLOCKS)
            block_of = lax.broadcasted_iota(jnp.int32, (depth, width), 0) // width
            position = jnp.zeros((depth, width), jnp.int32)
            for b in range(BLOCKS):
                position = jnp.where(block_of == b, rank_ref[b], position)
            tiles[0] = jnp.where(position < mine, tiles[0].astype(jnp.float32), 0.0).astype(jnp.bfloat16)
        tile = jnp.concatenate(tiles, axis=1) if pair > 1 else tiles[0]
        product = jnp.dot(error_ref[...], tile, preferred_element_type=jnp.float32)
        for i in range(pair):
            fresh = weight_ref[i] - product[:, i * width:(i + 1) * width]
            if own and i == 0:
                groups = code_ref.shape[1] // BLOCKS
                kept = keep_mask(code_ref[...], jnp.minimum(column, BLOCKS - 1) * groups, width)
                fresh = jnp.where(pruned, kept * fresh, fresh)
            out_ref[i] = fresh

    if first == 0:
        pl.when(pl.program_id(0) == 0)(lambda: run(True))
        pl.when(pl.program_id(0) > 0)(lambda: run(False))
    else:
        run(False)


def update(rank, errors, weight, factor, codes, first, so_far):
    laps, depth, width = factor.shape
    rows = weight.shape[1]
    pair = 2 if laps % 2 == 0 and first % 2 == 0 else 1
    if so_far is None:
        extra, extra_specs, aliases = [], [], {}
    else:
        extra, extra_specs, aliases = [so_far], [pl.BlockSpec(memory_space=pl.ANY)], {5: 0}
    return pl.pallas_call(
        functools.partial(update_kernel, first, pair),
        grid=(laps // pair,),
        out_shape=jax.ShapeDtypeStruct(weight.shape, weight.dtype),
        in_specs=[
            pl.BlockSpec(memory_space=pltpu.SMEM),
            pl.BlockSpec(memory_space=pltpu.VMEM),
            pl.BlockSpec((pair, rows, width), lambda i: (first // pair + i, 0, 0)),
            pl.BlockSpec((pair, depth, width), lambda i: (i, 0, 0)),
            pl.BlockSpec(memory_space=pltpu.VMEM),
        ] + extra_specs,
        out_specs=pl.BlockSpec((pair, rows, width), lambda i: (first // pair + i, 0, 0)),
        input_output_aliases=aliases,
        compiler_params=pltpu.CompilerParams(vmem_limit_bytes=40 << 20),
        cost_estimate=pl.CostEstimate(
            flops=2 * rows * depth * width * laps,
            bytes_accessed=laps * width * (8 * rows + 2 * depth),
            transcendentals=0,
        ),
        name="update",
    )(rank, errors, weight, factor, codes, *extra)


def body(weight, factor_rows, diag_inverse, keep_codes, block_order):
    columns = lax.axis_size("cols")
    column = lax.axis_index("cols").astype(jnp.int32)
    rows, laps, width = weight.shape
    part = rows // columns
    laps_first = weight.transpose(1, 0, 2)
    factor = factor_rows.transpose(1, 0, 2)

    spots = jnp.arange(BLOCKS, dtype=jnp.int32)
    rank = jnp.sum(jnp.where(block_order[None, :] == spots[:, None], spots[None, :], 0), axis=1)
    rank = jnp.concatenate([rank, column[None]]).astype(jnp.int32)

    factor_head = lax.all_gather(factor[0], ("cols", "rows"), axis=0, tiled=True)
    factor_head = factor_head.reshape(columns, -1, width)[:BLOCKS]
    head = lax.all_to_all(
        laps_first[0].reshape(columns, part, width), "cols", 0, 0, tiled=True
    )[:BLOCKS]
    my_codes = lax.dynamic_slice_in_dim(keep_codes, column * part, part, 0)
    my_errors = chain(block_order, head, factor_head, diag_inverse, my_codes)
    errors = lax.all_gather(my_errors, "cols", axis=0, tiled=True)

    half = max(2, (laps * 2 // 3) // 2 * 2)
    out = None
    for first, last in ((0, half), (half, laps)):
        chunk = lax.all_gather(factor[first:last], "rows", axis=1, tiled=True)
        out = update(rank, errors, laps_first, chunk, keep_codes, first, out)
    return out.transpose(1, 0, 2)


def solution(mesh):
    in_specs = (P("rows", None, "cols"), P("rows", None, "cols"), P(), P("rows", None), P())
    out_specs = P("rows", None, "cols")
    return jax.shard_map(body, mesh=mesh, in_specs=in_specs, out_specs=out_specs, check_vma=False)
```

time: 749 us -> 267 us (0.36)
  waiting for transfers between devices: 386 us -> 191 us
  matrix products: 188 us -> 0 us
  local copies, waits for them, and re-layouts: 78.6 us -> 19.9 us
  between operations: 59.5 us -> 13.2 us
  Pallas kernels: 0 us -> 36.7 us
  other arithmetic: 29.6 us -> 0.19 us
    psum x8 -> x0, waiting for transfers between devices: 360 us -> none  [spread(): return lax.psum(jnp.where(mine, shard, jnp.zeros_like(shard)), axis)]
    dot_general x24 -> x0, matrix products: 188 us -> none  [the longest x8 154 us: body(): jnp.dot(errors_bf, factor_tile.reshape(tile_width, -1), preferred_element...]
    all_gather x1 -> x4, waiting for transfers between devices: 24.9 us -> 176 us  [the longest x2 103 us: body(): chunk = lax.all_gather(factor[first:last], 'rows', axis=1, tiled=True)]
    reshape x16 -> x0, local copies, waits for them, and re-layouts: 36.7 us -> none  [decode(): return kept_mask.reshape(codes.shape[0], -1)]
    pallas_call x0 -> x3, Pallas kernels: none -> 36.7 us  [the longest x2 29.6 us: update(): pl.pallas_call(functools.partial(update_kernel, first, pair), grid=(laps...]
    dynamic_update_slice x8 -> x0, other arithmetic: 18.5 us -> none  [body(): lax.dynamic_update_index_in_dim(matrix, jnp.where(holder_here, kept_block...]
    dynamic_slice x9 -> x1, local copies, waits for them, and re-layouts: 16.6 us -> 0.02 us  [body(): my_codes = lax.dynamic_slice_in_dim(keep_codes, column * part, part, 0)]
    all_to_all x0 -> x1, waiting for transfers between devices: none -> 15.8 us  [body(): lax.all_to_all(laps_first[0].reshape(columns, part, width), 'cols', 0, 0,...]
  transfers between devices with their start and end apart: 9 -> 5, of which waited for: 8 -> 5; matrix products, arithmetic and copies ran while one was open for 12% -> 3% of each run, Pallas kernels for 0% -> 9%
where the time goes in v1:
time: 267 us
  waiting for transfers between devices  191 us (72%)
  Pallas kernels  36.7 us (14%)
  local copies, waits for them, and re-layouts  19.9 us (7%)
  between operations  13.2 us (5%)
  starting transfers between devices  5.29 us (2%)
    all_gather x2, waiting for transfers between devices, body(): chunk = lax.all_gather(factor[first:last], 'rows', axis=1, tiled=True)  103 us
    all_gather x1, waiting for transfers between devices, body(): errors = lax.all_gather(my_errors, 'cols', axis=0, tiled=True)  37.2 us
    all_gather x1, waiting for transfers between devices, body(): lax.all_gather(factor[0], ('cols', 'rows'), axis=0, tiled=True)  35.8 us
    pallas_call x2, Pallas kernels, update(): pl.pallas_call(functools.partial(update_kernel, first, pair), grid=(laps...  29.6 us
    all_to_all x1, waiting for transfers between devices, body(): lax.all_to_all(laps_first[0].reshape(columns, part, width), 'cols', 0, 0,...  15.8 us
    unnamed x18, local copies, waits for them, and re-layouts  11.7 us
    pallas_call x1, Pallas kernels, chain(): pl.pallas_call(chain_kernel, out_shape=jax.ShapeDtypeStruct((rows, BLOCKS...  7.07 us
  transfers between devices with their start and end apart: 5, of which 5 were waited for; matrix products, arithmetic and copies ran while one was open for 3% of the time, Pallas kernels for 9%

profile of v1, /device:TPU:0, one launch (start us, length us, event | category | flops | bytes accessed | tf_op | source)
XLA Modules:
  0.0 266.7 jit_solution(14627074217375751316)
XLA Ops:
  6.5 0.0 all-gather.12.cloned.1.call-start
  6.5 1.6 slice.17
  8.2 0.0 all-gather.12.cloned.1.call-update
  8.2 0.0 all-gather.10.cloned.1.call-start
  8.2 2.3 slice.19
  10.5 0.0 all-gather.10.cloned.1.call-update
  10.5 2.3 slice.16
  12.8 5.2 %all-to-all-start = ((f32[8,256,128]{2,1,0:T(8,128)}), f32[8,256,128]{2,1,0:T(8,128)S(1)}, u32[]{:S(2)}, u32[]{:S(2)}) async-start(f32[8,256,128]{2,1,0:T(8,128)} %bitcast.10), calls=%async_computation | async-start | bytes 2097152 | tf_op jit(solution)/shard_map/all_to_all | solution.py:147
  18.0 0.0 all-gather.6.cloned.1.call-start
  18.0 0.0 copy-done.2
  18.1 15.8 %all-to-all-done.block_ref = f32[8,256,128]{2,1,0:T(8,128)S(1)} async-done(((f32[8,256,128]{2,1,0:T(8,128)}), f32[8,256,128]{2,1,0:T(8,128)S(1)}, u32[]{:S(2)}, u32[]{:S(2)}) %all-to-all-start) | async-done | bytes 1048608 | tf_op jit(solution)/shard_map/all_to_all | solution.py:147
  33.8 35.8 %all-gather.12.cloned.1.call-done = bf16[1,8192,128]{2,1,0:T(8,128)(2,1)} async-done(((bf16[1,256,128]{2,1,0:T(8,128)(2,1)}), bf16[1,8192,128]{2,1,0:T(8,128)(2,1)}) %all-gather.12.cloned.1.call-update) | async-done | bytes 2097168 | tf_op jit(solution)/shard_map/all_gather | solution.py:145
  69.7 1.6 copy-done.6
  71.3 1.0 copy-done.7
  72.3 7.1 %chain.1 = bf16[256,1024]{1,0:T(8,128)(2,1)S(1)} custom-call(s32[8]{0:T(128)S(1)} %copy-done.8, f32[8,256,128]{2,1,0:T(8,128)S(1)} %all-to-all-done.block_ref, bf16[8,1024,128]{2,1,0:T(8,128)(2,1)S(1)} %bitcast.6, f32[8,128,128]{2,1,0:T(8,128)S(1)} %copy-done.7, s32[256,256]{1,0:T(8,128)S(1)} %constant_dynamic-slice_fusion.code_ref), custom_call_target="tpu_custom_call" | custom-call | tf_op jit(solution)/shard_map/chain/pallas_call | solution.py:58
  79.4 0.0 copy-start.5
  79.4 0.8 copy-done.5
  80.2 0.0 all-gather.6.cloned.1.call-update
  80.2 0.0 all-gather.8.cloned.1.call-start
  80.2 2.0 slice.18
  82.2 0.0 all-gather.8.cloned.1.call-update
  82.3 0.1 select_reduce_fusion
  82.4 0.1 pad_add_fusion.rank_ref
  82.5 68.4 %all-gather.10.cloned.1.call-done.factor_ref = bf16[16,1024,128]{2,1,0:T(8,128)(2,1)} async-done(((bf16[16,256,128]{2,1,0:T(8,128)(2,1)}), bf16[16,1024,128]{2,1,0:T(8,128)(2,1)}) %all-gather.10.cloned.1.call-update) | async-done | bytes 4194320 | tf_op jit(solution)/shard_map/all_gather | solution.py:157
  150.9 37.2 %all-gather.6.cloned.1.call-done.error_ref = bf16[2048,1024]{1,0:T(8,128)(2,1)} async-done(((bf16[256,1024]{1,0:T(8,128)(2,1)}), bf16[2048,1024]{1,0:T(8,128)(2,1)}) %all-gather.6.cloned.1.call-update) | async-done | bytes 4194320 | tf_op jit(solution)/shard_map/all_gather | solution.py:152
  188.1 2.2 copy-done
  190.2 2.2 copy-done.3
  192.4 17.7 %update.2.rest_0_ = f32[26,2048,128]{2,1,0:T(8,128)} custom-call(s32[9]{0:T(128)S(1)} %pad_add_fusion.rank_ref, bf16[2048,1024]{1,0:T(8,128)(2,1)S(1)} %copy-done, f32[26,2048,128]{2,1,0:T(8,128)} %bitcast.8, bf16[16,1024,128]{2,1,0:T(8,128)(2,1)S(1)} %copy-done.3, s32[2048,256]{1,0:T(8,128)S(1)} %copy-done.2), custom_call_target="tpu_custom_call" | custom-call | flops 8589934592 | bytes 37748736 | tf_op jit(solution)/shard_map/update/pallas_call | solution.py:110
  210.2 34.1 %all-gather.8.cloned.1.call-done.factor_ref = bf16[10,1024,128]{2,1,0:T(8,128)(2,1)} async-done(((bf16[10,256,128]{2,1,0:T(8,128)(2,1)}), bf16[10,1024,128]{2,1,0:T(8,128)(2,1)}) %all-gather.8.cloned.1.call-update) | async-done | bytes 2621456 | tf_op jit(solution)/shard_map/all_gather | solution.py:157
  244.3 2.2 copy-done.1
  246.5 1.7 copy-done.4
  248.2 11.9 %update.3 = f32[26,2048,128]{2,1,0:T(8,128)} custom-call(s32[9]{0:T(128)S(1)} %pad_add_fusion.rank_ref, bf16[2048,1024]{1,0:T(8,128)(2,1)S(1)} %copy-done.1, f32[26,2048,128]{2,1,0:T(8,128)} %bitcast.9, bf16[10,1024,128]{2,1,0:T(8,128)(2,1)S(1)} %copy-done.4, s32[2048,256]{1,0:T(8,128)S(1)} %copy-done.2, ...), custom_call_target="tpu_custom_call", output_to_operand_aliasing={{}: (5, {})} | custom-call | flops 5368709120 | bytes 23592960 | tf_op jit(solution)/shard_map/update/pallas_call | solution.py:110
  (10 shorter events, 0.0 us)
Async XLA Ops:
  6.5 11.5 %copy-start.2 = (s32[2048,256]{1,0:T(8,128)S(1)}, s32[2048,256]{1,0:T(8,128)}, u32[]{:S(2)}) copy-start(s32[2048,256]{1,0:T(8,128)} %code_ref.3) | copy-start | bytes 6291460
  6.5 63.1 %copy-start.8 = (s32[8]{0:T(128)S(1)}, s32[8]{0:T(128)}, u32[]{:S(2)}) copy-start(s32[8]{0:T(128)} %order_ref.1) | copy-start | bytes 100
  6.5 63.1 %all-gather.12.cloned.1.call-start = ((), (), s32[]{:S(2)}) async-start(), calls=%async_computation.4 | async-start | bytes 2162688 | tf_op jit(solution)/shard_map/all_gather | solution.py:145
  8.2 142.7 %all-gather.10.cloned.1.call-start = ((), (), s32[]{:S(2)}) async-start(), calls=%async_computation.3 | async-start | bytes 5242880 | tf_op jit(solution)/shard_map/all_gather | solution.py:157
  12.8 21.0 %all-to-all-start = ((f32[8,256,128]{2,1,0:T(8,128)}), f32[8,256,128]{2,1,0:T(8,128)S(1)}, u32[]{:S(2)}, u32[]{:S(2)}) async-start(f32[8,256,128]{2,1,0:T(8,128)} %bitcast.10), calls=%async_computation | async-start | bytes 2097152 | tf_op jit(solution)/shard_map/all_to_all | solution.py:147
  18.0 170.1 %all-gather.6.cloned.1.call-start = ((), (), s32[]{:S(2)}) async-start(), calls=%async_computation.1 | async-start | bytes 4718592 | tf_op jit(solution)/shard_map/all_gather | solution.py:152
  69.7 1.6 copy-start.6
  71.3 1.0 copy-start.7
  79.4 0.8 copy-start.5
  80.2 164.1 %all-gather.8.cloned.1.call-start = ((), (), s32[]{:S(2)}) async-start(), calls=%async_computation.2 | async-start | bytes 3276800 | tf_op jit(solution)/shard_map/all_gather | solution.py:157
  188.1 2.2 copy-start
  190.2 2.2 copy-start.3
  244.3 2.2 copy-start.1
  246.5 1.7 copy-start.4
Sparse Core Ops, SparseCore 0:
  10.3 59.3 all-gather.11
  71.2 79.6 all-gather.9
  152.8 35.2 all-gather.5
  189.5 54.7 all-gather.7

commit v2 on v0

v2 whole, which is shorter than its diff:
```python
import functools

import jax
import jax.numpy as jnp
from jax import lax
from jax.experimental import pallas as pl
from jax.experimental.pallas import tpu as pltpu
from jax.sharding import PartitionSpec as P

BLOCKS = 8
GROUP = 4


def keep_mask(codes, first_group, width):
    groups = codes.shape[1]
    row = lax.broadcasted_iota(jnp.int32, (groups, width), 0)
    column = lax.broadcasted_iota(jnp.int32, (groups, width), 1)
    pick = (row == first_group + column // GROUP).astype(jnp.float32).astype(jnp.bfloat16)
    spread_codes = jnp.dot(
        codes.astype(jnp.float32).astype(jnp.bfloat16), pick, preferred_element_type=jnp.float32
    )
    place = lax.broadcasted_iota(jnp.int32, (1, width), 1) % GROUP
    first = jnp.where(place < 2, 0.0, jnp.where(place == 2, 1.0, 2.0))
    second = jnp.where(place == 0, 1.0, jnp.where(place == 3, 4.0, 3.0))
    third = jnp.where(place == 0, 2.0, jnp.where(place == 1, 4.0, 5.0))
    hit = (spread_codes == first) | (spread_codes == second) | (spread_codes == third)
    return jnp.where(hit, 1.0, 0.0)


def chunk_ends(laps):
    bounds = [(0, 1)] if laps else []
    at = 1
    while at < laps:
        left = laps - at
        size = 6 if left >= 15 else 4 if left >= 7 else min(left, 3)
        bounds.append((at, at + size))
        at += size
    return bounds


def prune_kernel(
    n_rows, n_cols, order_ref, weight_ref, factor_ref, diag_ref, code_ref, out_ref,
    gathered, errors, heads, head_factor, by_step,
    factor_send, factor_recv, head_send, head_recv,
    spread_send, spread_recv, local_sem,
):
    laps, rows, width = weight_ref.shape
    depth = factor_ref.shape[1]
    part = rows // n_cols
    pairs = n_cols // 2
    groups = code_ref.shape[1] // BLOCKS
    bounds = chunk_ends(laps)
    count = len(bounds)
    z = lax.axis_index("rows")
    c = lax.axis_index("cols")
    partner = c + 1 - 2 * lax.rem(c, 2)

    def around(k):
        return lax.rem(c + k + n_cols, n_cols)

    def cut(index, size):
        return pl.ds(pl.multiple_of(index * size, size), size)

    barrier = pltpu.get_barrier_semaphore()
    for k in range(1, n_cols):
        pl.semaphore_signal(
            barrier, inc=1, device_id={"cols": around(k)}, device_id_type=pl.DeviceIdType.MESH
        )

    @pl.when(z > 0)
    def _():
        pl.semaphore_signal(
            barrier, inc=1, device_id={"rows": z - 1}, device_id_type=pl.DeviceIdType.MESH
        )

    @pl.when(z < n_rows - 1)
    def _():
        pl.semaphore_signal(
            barrier, inc=1, device_id={"rows": z + 1}, device_id_type=pl.DeviceIdType.MESH
        )

    below = jnp.where(z > 0, 1, 0)
    above = jnp.where(z < n_rows - 1, 1, 0)
    pl.semaphore_wait(barrier, n_cols - 1 + below + above)

    def factor_copy(q, source, up, own):
        low, high = bounds[q]
        place = gathered.at[pl.ds(low, high - low), cut(source, depth), :]
        return pltpu.make_async_remote_copy(
            src_ref=factor_ref.at[pl.ds(low, high - low)] if own else place,
            dst_ref=place,
            send_sem=factor_send.at[up, source, q],
            recv_sem=factor_recv.at[source, q],
            device_id={"rows": z + 1 if up else z - 1},
            device_id_type=pl.DeviceIdType.MESH,
        )

    def own(q):
        if q < count:
            pl.when(z > 0)(lambda: factor_copy(q, z, 0, True).start())
            pl.when(z < n_rows - 1)(lambda: factor_copy(q, z, 1, True).start())

    def hop(q, k):
        if q >= count or k >= n_rows:
            return

        @pl.when(z + k < n_rows)
        def _():
            factor_copy(q, z + k, 0, False).wait_recv()
            pl.when(z > 0)(lambda: factor_copy(q, z + k, 0, False).start())

        @pl.when(z - k >= 0)
        def _():
            factor_copy(q, z - k, 1, False).wait_recv()
            pl.when(z < n_rows - 1)(lambda: factor_copy(q, z - k, 1, False).start())

    def hops(q, first=1):
        for k in range(first, n_rows):
            hop(q, k)

    def head_copy(target, source):
        return pltpu.make_async_remote_copy(
            src_ref=weight_ref.at[0, cut(target, part), :],
            dst_ref=heads.at[source],
            send_sem=head_send.at[target],
            recv_sem=head_recv.at[source],
            device_id={"cols": target},
            device_id_type=pl.DeviceIdType.MESH,
        )

    def spread_copy(kind, source, target, slot):
        if kind == 0:
            block = head_factor.at[source]
        else:
            block = errors.at[cut(source, part), :]
        return pltpu.make_async_remote_copy(
            src_ref=block,
            dst_ref=block,
            send_sem=spread_send.at[kind, slot],
            recv_sem=spread_recv.at[kind, source],
            device_id={"cols": target},
            device_id_type=pl.DeviceIdType.MESH,
        )

    def spread_start(kind):
        for k in range(1, pairs):
            spread_copy(kind, c, around(2 * k), k).start()
        spread_copy(kind, c, partner, 0).start()

    def spread_forward(kind):
        for k in range(1, pairs):
            source = around(-2 * k)
            spread_copy(kind, source, partner, pairs + k).wait_recv()
            spread_copy(kind, source, partner, pairs + k).start()

    def spread_finish(kind):
        spread_copy(kind, partner, partner, 0).wait_recv()
        for k in range(1, pairs):
            spread_copy(kind, lax.rem(partner - 2 * k + n_cols, n_cols), partner, pairs + k).wait_recv()

    own(0)
    for k in range(1, n_cols):
        head_copy(around(k), c).start()
    own(1)
    own_head = pltpu.make_async_copy(weight_ref.at[0, cut(c, part), :], heads.at[c], local_sem.at[0])
    own_head.start()
    own_factor = pltpu.make_async_copy(factor_ref, gathered.at[:, cut(z, depth), :], local_sem.at[1])
    own_factor.start()
    fetch = pltpu.make_async_copy(weight_ref, out_ref, local_sem.at[2])
    fetch.start()

    hops(0)
    own_factor.wait()
    own(2)
    head_factor[c] = gathered[0].reshape(BLOCKS, width, width)
    spread_start(0)
    own_head.wait()
    for k in range(1, n_cols):
        head_copy(c, around(-k)).wait_recv()
    hop(1, 1)
    spread_forward(0)
    spread_finish(0)
    hop(1, 2)

    my_codes = code_ref.at[cut(c, part), :]

    def step(s, carry):
        b = order_ref[s]
        kept = keep_mask(my_codes[...], b * groups, width)
        fresh = jnp.dot(
            heads[b] * (1.0 - kept),
            diag_ref[b],
            precision=lax.Precision.HIGHEST,
            preferred_element_type=jnp.float32,
        ).astype(jnp.bfloat16)
        by_step[s] = fresh
        for t in range(BLOCKS):
            heads[t] = heads[t] - jnp.dot(fresh, head_factor[t, b], preferred_element_type=jnp.float32)
        return carry

    lax.fori_loop(0, BLOCKS, step, 0)

    rank = []
    for b in range(BLOCKS):
        at = 0
        for s in range(BLOCKS):
            at = at + jnp.where(order_ref[s] == b, s, 0)
        at = jnp.minimum(at, BLOCKS - 1)
        rank.append(at)
        errors[cut(c, part), b * width:(b + 1) * width] = by_step[at]

    spread_start(1)
    own(3)
    hops(1, 3)
    hop(2, 1)
    spread_forward(1)
    hop(2, 2)
    spread_finish(1)
    own(4)
    hops(2, 3)
    hop(3, 1)
    fetch.wait()

    tile_rows = min(rows, 512)

    def by_rows(work):
        lax.fori_loop(0, rows // tile_rows, lambda i, carry: work(cut(i, tile_rows)) or carry, 0)

    def first_lap():
        column = jnp.minimum(c, BLOCKS - 1)
        pruned = c < BLOCKS
        mine = BLOCKS
        for b in range(BLOCKS):
            mine = jnp.where(c == b, rank[b], mine)
        block_of = lax.broadcasted_iota(jnp.int32, (BLOCKS * width, width), 0) // width
        position = jnp.zeros((BLOCKS * width, width), jnp.int32)
        for b in range(BLOCKS):
            position = jnp.where(block_of == b, rank[b], position)
        tile = jnp.where(position < mine, gathered[0].astype(jnp.float32), 0.0).astype(jnp.bfloat16)

        def work(at):
            product = jnp.dot(errors[at, :], tile, preferred_element_type=jnp.float32)
            fresh = out_ref[0, at, :] - product
            kept = keep_mask(code_ref[at, :], column * groups, width)
            out_ref[0, at, :] = jnp.where(pruned, kept * fresh, fresh)

        by_rows(work)

    def laps_at(lap, many):
        tile = [gathered[lap + i] for i in range(many)]
        tile = jnp.concatenate(tile, axis=1) if many > 1 else tile[0]

        def work(at):
            product = jnp.dot(errors[at, :], tile, preferred_element_type=jnp.float32)
            for i in range(many):
                out_ref[lap + i, at, :] = out_ref[lap + i, at, :] - product[:, i * width:(i + 1) * width]

        by_rows(work)

    def compute(q):
        low, high = bounds[q]
        if q == 0:
            first_lap()
            return
        twos = (high - low) // 2
        lax.fori_loop(0, twos, lambda i, carry: laps_at(low + 2 * i, 2) or carry, 0)
        if (high - low) % 2:
            laps_at(high - 1, 1)

    compute(0)
    hop(3, 2)
    compute(1)
    hops(3, 3)
    own(5)
    hop(4, 1)
    compute(2)
    for q in range(3, count):
        own(q + 3)
        hops(q + 1, 2)
        hop(q + 2, 1)
        compute(q)

    for q in range(count):
        for source in range(n_rows):
            pl.when((z > 0) & (z <= source))(lambda: factor_copy(q, source, 0, False).wait_send())
            pl.when((z < n_rows - 1) & (z >= source))(lambda: factor_copy(q, source, 1, False).wait_send())
    for k in range(1, n_cols):
        head_copy(around(k), c).wait_send()
    for kind in range(2):
        for slot in range(2 * pairs):
            if slot != pairs:
                spread_copy(kind, c, partner, slot).wait_send()


def store_kernel(kept_ref, out_ref, sems):
    laps = kept_ref.shape[0]
    copies = [pltpu.make_async_copy(kept_ref.at[l], out_ref.at[l], sems.at[l]) for l in range(laps)]
    for copy in copies:
        copy.start()
    for copy in copies:
        copy.wait()


def store(kept):
    return pl.pallas_call(
        store_kernel,
        out_shape=jax.ShapeDtypeStruct(kept.shape, kept.dtype),
        in_specs=[pl.BlockSpec(memory_space=pltpu.VMEM)],
        out_specs=pl.BlockSpec(memory_space=pl.ANY),
        scratch_shapes=[pltpu.SemaphoreType.DMA((kept.shape[0],))],
        compiler_params=pltpu.CompilerParams(vmem_limit_bytes=1 << 20),
        name="store",
    )(kept)


def body(weight, factor_rows, diag_inverse, keep_codes, block_order):
    n_rows, n_cols = lax.axis_size("rows"), lax.axis_size("cols")
    rows, laps, width = weight.shape
    part = rows // n_cols
    depth = factor_rows.shape[0] * n_rows
    count = len(chunk_ends(laps))
    anywhere = pl.BlockSpec(memory_space=pl.ANY)
    inside = pl.BlockSpec(memory_space=pltpu.VMEM)
    dma = pltpu.SemaphoreType.DMA
    out = pl.pallas_call(
        functools.partial(prune_kernel, n_rows, n_cols),
        out_shape=pltpu.VMEM((laps, rows, width), jnp.float32),
        in_specs=[pl.BlockSpec(memory_space=pltpu.SMEM), anywhere, anywhere, inside, inside],
        out_specs=inside,
        scratch_shapes=[
            pltpu.VMEM((laps, depth, width), jnp.bfloat16),
            pltpu.VMEM((rows, BLOCKS * width), jnp.bfloat16),
            pltpu.VMEM((n_cols, part, width), jnp.float32),
            pltpu.VMEM((n_cols, BLOCKS, width, width), jnp.bfloat16),
            pltpu.VMEM((BLOCKS, part, width), jnp.bfloat16),
            dma((2, n_rows, count)),
            dma((n_rows, count)),
            dma((n_cols,)),
            dma((n_cols,)),
            dma((2, n_cols)),
            dma((2, n_cols)),
            dma((3,)),
        ],
        compiler_params=pltpu.CompilerParams(
            collective_id=0, has_side_effects=True, vmem_limit_bytes=30 << 20
        ),
        cost_estimate=pl.CostEstimate(
            flops=2 * rows * depth * width * laps,
            bytes_accessed=laps * width * (8 * rows + 2 * depth),
            transcendentals=0,
        ),
        name="prune",
    )(
        block_order,
        weight.transpose(1, 0, 2),
        factor_rows.transpose(1, 0, 2),
        diag_inverse,
        keep_codes,
    )
    return store(out).transpose(1, 0, 2)


def solution(mesh):
    in_specs = (P("rows", None, "cols"), P("rows", None, "cols"), P(), P("rows", None), P())
    out_specs = P("rows", None, "cols")
    return jax.shard_map(body, mesh=mesh, in_specs=in_specs, out_specs=out_specs, check_vma=False)
```

time: 749 us -> 142 us (0.19)
  waiting for transfers between devices: 386 us -> 0 us
  matrix products: 188 us -> 0 us
  Pallas kernels: 0 us -> 142 us
  local copies, waits for them, and re-layouts: 78.6 us -> 0 us
  between operations: 59.5 us -> 0.01 us
  other arithmetic: 29.6 us -> 0 us
    psum x8 -> x0, waiting for transfers between devices: 360 us -> none  [spread(): return lax.psum(jnp.where(mine, shard, jnp.zeros_like(shard)), axis)]
    dot_general x24 -> x0, matrix products: 188 us -> none  [the longest x8 154 us: body(): jnp.dot(errors_bf, factor_tile.reshape(tile_width, -1), preferred_element...]
    pallas_call x0 -> x2, Pallas kernels: none -> 142 us  [the longest x1 133 us: body(): pl.pallas_call(functools.partial(prune_kernel, n_rows, n_cols), out_shape...]
    reshape x16 -> x0, local copies, waits for them, and re-layouts: 36.7 us -> none  [decode(): return kept_mask.reshape(codes.shape[0], -1)]
    all_gather x1 -> x0, waiting for transfers between devices: 24.9 us -> none  [body(): all_factor = lax.all_gather(factor_rows, 'rows', axis=0, tiled=True)]
    unnamed x28 -> x0, local copies, waits for them, and re-layouts: 24.6 us -> none
    dynamic_update_slice x8 -> x0, other arithmetic: 18.5 us -> none  [body(): lax.dynamic_update_index_in_dim(matrix, jnp.where(holder_here, kept_block...]
    dynamic_slice x9 -> x0, local copies, waits for them, and re-layouts: 16.6 us -> none  [errors(): lax.dynamic_slice_in_dim(keep_codes, block_now * 32, 32, 1)]
  transfers between devices with their start and end apart: 9 -> 0, of which waited for: 8 -> 0; matrix products, arithmetic and copies ran while one was open for 12% -> 0% of each run, Pallas kernels for 0% -> 0%
where the time goes in v2:
time: 142 us
  Pallas kernels  142 us (100%)
    pallas_call x1, Pallas kernels, body(): pl.pallas_call(functools.partial(prune_kernel, n_rows, n_cols), out_shape...  133 us
    pallas_call x1, Pallas kernels, store(): pl.pallas_call(store_kernel, out_shape=jax.ShapeDtypeStruct(kept.shape, k...  9.2 us

profile of v2, /device:TPU:0, one launch (start us, length us, event | category | flops | bytes accessed | tf_op | source)
XLA Modules:
  0.0 142.2 jit_solution(15156627890837848301)
XLA Ops:
  0.0 133.0 %prune.1.kept_ref = f32[26,2048,128]{2,1,0:T(8,128)S(1)} custom-call(s32[8]{0:T(128)} %order_ref.1, f32[26,2048,128]{2,1,0:T(8,128)} %bitcast.3, bf16[26,256,128]{2,1,0:T(8,128)(2,1)} %bitcast.4, f32[8,128,128]{2,1,0:T(8,128)} %diag_ref.1, s32[2048,256]{1,0:T(8,128)} %code_ref.1), custom_call_target="tpu_custom_call" | custom-call | flops 13958643712 | bytes 61341696 | tf_op jit(solution)/shard_map/prune/pallas_call | solution.py:325
  133.0 9.2 %store.1 = f32[26,2048,128]{2,1,0:T(8,128)} custom-call(f32[26,2048,128]{2,1,0:T(8,128)S(1)} %prune.1.kept_ref), custom_call_target="tpu_custom_call" | custom-call | tf_op jit(solution)/shard_map/store/pallas_call | solution.py:305

commit v3 on v2

--- a/solution.py
+++ b/solution.py
@@ -114,9 +114,13 @@
             factor_copy(q, z - k, 1, False).wait_recv()
             pl.when(z < n_rows - 1)(lambda: factor_copy(q, z - k, 1, False).start())
 
-    def hops(q, first=1):
-        for k in range(first, n_rows):
+    def middle(q):
+        for k in range(2, n_rows - 1):
             hop(q, k)
+
+    def last(q):
+        if n_rows > 2:
+            hop(q, n_rows - 1)
 
     def head_copy(target, source):
         return pltpu.make_async_remote_copy(
@@ -161,7 +165,6 @@
     own(0)
     for k in range(1, n_cols):
         head_copy(around(k), c).start()
-    own(1)
     own_head = pltpu.make_async_copy(weight_ref.at[0, cut(c, part), :], heads.at[c], local_sem.at[0])
     own_head.start()
     own_factor = pltpu.make_async_copy(factor_ref, gathered.at[:, cut(z, depth), :], local_sem.at[1])
@@ -169,18 +172,21 @@
     fetch = pltpu.make_async_copy(weight_ref, out_ref, local_sem.at[2])
     fetch.start()
 
-    hops(0)
+    hop(0, 1)
+    middle(0)
+    last(0)
+    own(1)
+    own(2)
+    own(3)
     own_factor.wait()
-    own(2)
     head_factor[c] = gathered[0].reshape(BLOCKS, width, width)
     spread_start(0)
     own_head.wait()
     for k in range(1, n_cols):
         head_copy(c, around(-k)).wait_recv()
+    spread_forward(0)
     hop(1, 1)
-    spread_forward(0)
     spread_finish(0)
-    hop(1, 2)
 
     my_codes = code_ref.at[cut(c, part), :]
 
@@ -210,15 +216,15 @@
         errors[cut(c, part), b * width:(b + 1) * width] = by_step[at]
 
     spread_start(1)
-    own(3)
-    hops(1, 3)
     hop(2, 1)
+    own(4)
+    middle(1)
+    hop(3, 1)
     spread_forward(1)
-    hop(2, 2)
+    own(5)
+    middle(2)
     spread_finish(1)
-    own(4)
-    hops(2, 3)
-    hop(3, 1)
+    last(1)
     fetch.wait()
 
     tile_rows = min(rows, 512)
@@ -268,16 +274,17 @@
             laps_at(high - 1, 1)
 
     compute(0)
-    hop(3, 2)
     compute(1)
-    hops(3, 3)
-    own(5)
+    own(6)
+    middle(3)
     hop(4, 1)
+    last(2)
     compute(2)
     for q in range(3, count):
-        own(q + 3)
-        hops(q + 1, 2)
+        own(q + 4)
+        middle(q + 1)
         hop(q + 2, 1)
+        last(q)
         compute(q)
 
     for q in range(count):

time: 142 us -> 137 us (0.965)
  Pallas kernels: 142 us -> 136 us
    pallas_call x1, Pallas kernels: 133 us -> 127 us  [body(): pl.pallas_call(functools.partial(prune_kernel, n_rows, n_cols), out_shape...]
where the time goes in v3:
time: 137 us; the launch traced here: 136 us
  Pallas kernels  136 us (99%)
    pallas_call x1, Pallas kernels, body(): pl.pallas_call(functools.partial(prune_kernel, n_rows, n_cols), out_shape...  127 us
    pallas_call x1, Pallas kernels, store(): pl.pallas_call(store_kernel, out_shape=jax.ShapeDtypeStruct(kept.shape, k...  9.2 us

profile of v3, /device:TPU:0, one launch (start us, length us, event | category | flops | bytes accessed | tf_op | source)
XLA Modules:
  0.0 136.4 jit_solution(3727851659235209677)
XLA Ops:
  0.0 127.2 %prune.1.kept_ref = f32[26,2048,128]{2,1,0:T(8,128)S(1)} custom-call(s32[8]{0:T(128)} %order_ref.1, f32[26,2048,128]{2,1,0:T(8,128)} %bitcast.3, bf16[26,256,128]{2,1,0:T(8,128)(2,1)} %bitcast.4, f32[8,128,128]{2,1,0:T(8,128)} %diag_ref.1, s32[2048,256]{1,0:T(8,128)} %code_ref.1), custom_call_target="tpu_custom_call" | custom-call | flops 13958643712 | bytes 61341696 | tf_op jit(solution)/shard_map/prune/pallas_call | solution.py:332
  127.2 9.2 %store.1 = f32[26,2048,128]{2,1,0:T(8,128)} custom-call(f32[26,2048,128]{2,1,0:T(8,128)S(1)} %prune.1.kept_ref), custom_call_target="tpu_custom_call" | custom-call | tf_op jit(solution)/shard_map/store/pallas_call | solution.py:312
